TPU v7x, 128 devices: a whole 4x4x4 slice. The times are simulated.
128 devices in a mesh: dom: 8 (over z, core), grp: 16 (over x, y).
Axes of the slice: x: 4, y: 4, z: 4, core: 2. Of those that a mesh axis runs over, the one named last changes fastest.
Arguments:
- inputs: bfloat16 [393216, 256], P(('dom', 'grp')), may hold values from -6 to 6
- initial: bfloat16 [393216, 256], P(('dom', 'grp')), may hold values from -6 to 6
- history: bfloat16 [393216, 256], P(('dom', 'grp')), may hold values from -6 to 6
- upstream: bfloat16 [393216, 256], P(('dom', 'grp')), may hold values from -6 to 6
- weight: bfloat16 [256, 256], replicated, may hold values from -0.375 to 0.375
- tile_vals: bfloat16 [36864, 128, 128], P(('dom', 'grp')), may hold values from 0 to 0.088378906
- tile_row: int32 [36864], P(('dom', 'grp')), may hold values from 0 to 23
- tile_col: int32 [36864], P(('dom', 'grp')), may hold values from 0 to 47, as said below
- tile_count: int32 [128], P(('dom', 'grp')), may hold values from 48 to 288, as said below
- send_rows: int32 [8, 16, 128, 8], P('dom', 'grp'), may hold values from 0 to 3071
- cache_ask: int32 [8, 16, 8, 2], P('dom', 'grp'), may hold values from 0 to 23
Outputs:
- layer_out: bfloat16 [393216, 256], P(('dom', 'grp'))
- grad_inputs: float32 [393216, 256], P(('dom', 'grp'))
- grad_weight: float32 [256, 256], replicated
Inputs may be any that keep to these rules, and one draw needn't show every extreme that they name: `send_rows`: row numbers within the sending section. `cache_ask`: block numbers within the owning section. `tile_row`: row block within the section. `tile_col`: in each section's list the first 48 tiles name every column block once. `tile_count`: some section has exactly 288 live tiles.
All inputs are finite; a program needn't handle non-finite values.
Results may differ from a plain program's by a relative error of at most 0.0053.
Values may be sent and summed in bfloat16 or wider, within the bound.
A program may use at most 128 MiB of HBM per device.

v0:
```python
import math

import jax
import jax.numpy as jnp
from jax import lax
from jax.sharding import PartitionSpec as P

alpha_res = 0.1
beta_map = 0.4


def silu_slope(pre_act):
    squash = jax.nn.sigmoid(pre_act)
    return squash * (1.0 + pre_act * (1.0 - squash))


def turn_width(slot_count):
    for option_width in (96, 48, 32, 16, 8):
        return option_width
    return slot_count


def per_device(
    inputs,
    initial,
    history,
    upstream,
    weight,
    tile_vals,
    tile_row,
    tile_col,
    tile_count,
    send_rows,
    cache_ask,
):
    row_count, feature_dim = inputs.shape
    block_rows = tile_vals.shape[1]
    block_count = row_count // block_rows
    slot_count = tile_vals.shape[0]
    group_size = turn_width(slot_count)
    dom_count = lax.axis_size("dom")
    grp_count = lax.axis_size("grp")
    peer_count = dom_count * grp_count
    send_list = send_rows.reshape(peer_count, -1)
    per_peer = send_list.shape[1]
    ask_list = cache_ask.reshape(dom_count, -1)
    asked_per = ask_list.shape[1]
    outgoing = inputs[send_list.reshape(-1)].reshape(peer_count, per_peer, feature_dim)
    arrived = lax.all_to_all(outgoing, ("dom", "grp"), split_axis=0, concat_axis=0, tiled=True)
    arrived = arrived.reshape(peer_count * per_peer, feature_dim)
    wanted = lax.all_to_all(ask_list, "dom", split_axis=0, concat_axis=0, tiled=True)
    own_blocks = history.reshape(block_count, block_rows, feature_dim)
    served = own_blocks[wanted.reshape(-1)].reshape(dom_count, asked_per * block_rows, feature_dim)
    cached = lax.all_to_all(served, "dom", split_axis=0, concat_axis=0, tiled=True)
    cached = cached.reshape(dom_count * asked_per * block_rows, feature_dim)
    columns = jnp.concatenate([inputs, arrived, cached], axis=0)
    col_blocks = columns.reshape(-1, block_rows, feature_dim)
    column_total = col_blocks.shape[0]
    live_count = tile_count[0]
    turn_count = (live_count + group_size - 1) // group_size

    def turn_slices(turn_index):
        offset = turn_index * group_size
        tile_block = lax.dynamic_slice_in_dim(tile_vals, offset, group_size, 0)
        row_pick = lax.dynamic_slice_in_dim(tile_row, offset, group_size, 0)
        col_pick = lax.dynamic_slice_in_dim(tile_col, offset, group_size, 0)
        live_part = (offset + jnp.arange(group_size) < live_count).astype(jnp.float32)
        return (tile_block, row_pick, col_pick, live_part)

    def forward_turn(turn_index, totals):
        tile_block, row_pick, col_pick, live_part = turn_slices(turn_index)
        products = jnp.einsum(
            "tij,tjd->tid", tile_block, col_blocks[col_pick], preferred_element_type=jnp.float32
        )
        placing = (row_pick[:, None] == jnp.arange(block_count)[None, :]).astype(
            jnp.float32
        ) * live_part[:, None]
        return totals + jnp.einsum(
            "tr,tid->rid", placing, products, precision=lax.Precision.HIGHEST
        )

    gathered = lax.fori_loop(
        0, turn_count, forward_turn, jnp.zeros((block_count, block_rows, feature_dim), jnp.float32)
    )
    mixture = (1.0 - alpha_res) * gathered.reshape(
        row_count, feature_dim
    ) + alpha_res * initial.astype(jnp.float32)
    mixed_b = mixture.astype(jnp.bfloat16)
    pre_act = (1.0 - beta_map) * mixture + beta_map * jnp.dot(
        mixed_b, weight, preferred_element_type=jnp.float32
    )
    layer_out = jax.nn.silu(pre_act).astype(jnp.bfloat16)
    act_slope = upstream.astype(jnp.float32) * silu_slope(pre_act)
    slope_b = act_slope.astype(jnp.bfloat16)
    weight_part = lax.dot_general(
        mixed_b, slope_b, (((0,), (0,)), ((), ())), preferred_element_type=jnp.float32
    )
    through_weight = lax.dot_general(
        slope_b, weight, (((1,), (1,)), ((), ())), preferred_element_type=jnp.float32
    )
    back_grad = (
        (1.0 - alpha_res) * ((1.0 - beta_map) * act_slope + beta_map * through_weight)
    ).astype(jnp.bfloat16)
    back_blocks = back_grad.reshape(block_count, block_rows, feature_dim)

    def backward_turn(turn_index, totals):
        tile_block, row_pick, col_pick, live_part = turn_slices(turn_index)
        spread = jnp.einsum(
            "tji,tjd->tid", tile_block, back_blocks[row_pick], preferred_element_type=jnp.float32
        )
        onto_mask = (col_pick[:, None] == jnp.arange(column_total)[None, :]).astype(
            jnp.float32
        ) * live_part[:, None]
        return totals + jnp.einsum(
            "tc,tid->cid", onto_mask, spread, precision=lax.Precision.HIGHEST
        )

    column_grads = lax.fori_loop(
        0,
        turn_count,
        backward_turn,
        jnp.zeros((column_total, block_rows, feature_dim), jnp.float32),
    )
    fresh_blocks = peer_count * per_peer // block_rows
    own_grads = column_grads[:block_count].reshape(row_count, feature_dim)
    fresh_grads = (
        column_grads[block_count : block_count + fresh_blocks]
        .reshape(peer_count, per_peer, feature_dim)
        .astype(jnp.bfloat16)
    )
    returned = lax.all_to_all(fresh_grads, ("dom", "grp"), split_axis=0, concat_axis=0, tiled=True)
    returned = returned.reshape(peer_count * per_peer, feature_dim).astype(jnp.float32)
    grad_inputs = own_grads.at[send_list.reshape(-1)].add(returned)
    weight_total = lax.psum(weight_part, ("dom", "grp"))
    grad_weight = weight_total * (beta_map / math.sqrt(row_count * peer_count))
    return (layer_out, grad_inputs, grad_weight)


def solution(mesh):
    placed = (
        P(("dom", "grp"), None),
        P(("dom", "grp"), None),
        P(("dom", "grp"), None),
        P(("dom", "grp"), None),
        P(),
        P(("dom", "grp"), None, None),
        P(("dom", "grp")),
        P(("dom", "grp")),
        P(("dom", "grp")),
        P("dom", "grp", None, None),
        P("dom", "grp", None, None),
    )
    return jax.shard_map(
        per_device,
        mesh=mesh,
        in_specs=placed,
        out_specs=(P(("dom", "grp"), None), P(("dom", "grp"), None), P()),
        check_vma=False,
    )
```

profile of v0, /device:TPU:1, one launch (start us, length us, event | category | flops | bytes accessed | tf_op | source)
XLA Modules:
  0.0 450.1 jit_solution(1641534458222594287)
XLA Ops:
  8.6 6.8 %all-to-all-start.1 = ((s32[8,1,2]{2,1,0:T(1,128)}), s32[8,1,2]{2,1,0:T(1,128)S(1)}, u32[]{:S(2)}, u32[]{:S(2)}) async-start(s32[8,1,2]{2,1,0:T(1,128)} %copy.25), calls=%async_computation.1 | async-start | bytes 8192 | tf_op jit(solution)/shard_map/all_to_all | solution.py:51
  17.0 6.2 %gather_fusion.2 = bf16[1024,256]{1,0:T(8,128)(2,1)} fusion(bf16[3072,256]{1,0:T(8,128)(2,1)} %param.15, s32[1024]{0:T(1024)S(1)} %broadcast_clamp_fusion), kind=kCustom, calls=%fused_computation.2 | custom fusion | bytes 1052672 | tf_op jit(solution)/shard_map/gather | solution.py:48
  23.2 9.9 %all-to-all-start = ((bf16[128,8,256]{2,1,0:T(8,128)(2,1)}), bf16[128,8,256]{2,1,0:T(8,128)(2,1)}, u32[]{:S(2)}, u32[]{:S(2)}) async-start(bf16[128,8,256]{2,1,0:T(8,128)(2,1)} %bitcast.49), calls=%async_computation | async-start | bytes 1048576 | tf_op jit(solution)/shard_map/all_to_all | solution.py:49
  36.0 10.1 %all-to-all-done = bf16[128,8,256]{2,1,0:T(8,128)(2,1)} async-done(((bf16[128,8,256]{2,1,0:T(8,128)(2,1)}), bf16[128,8,256]{2,1,0:T(8,128)(2,1)}, u32[]{:S(2)}, u32[]{:S(2)}) %all-to-all-start) | async-done | bytes 524320 | tf_op jit(solution)/shard_map/all_to_all | solution.py:49
  46.1 4.8 %all-to-all-start.2 = ((bf16[8,256,256]{2,1,0:T(8,128)(2,1)}), bf16[8,256,256]{2,1,0:T(8,128)(2,1)S(1)}, u32[]{:S(2)}, u32[]{:S(2)}) async-start(bf16[8,256,256]{2,1,0:T(8,128)(2,1)} %bitcast.46), calls=%async_computation.2 | async-start | bytes 2097152 | tf_op jit(solution)/shard_map/all_to_all | solution.py:54
  51.6 14.4 %all-to-all-done.2 = bf16[8,256,256]{2,1,0:T(8,128)(2,1)S(1)} async-done(((bf16[8,256,256]{2,1,0:T(8,128)(2,1)}), bf16[8,256,256]{2,1,0:T(8,128)(2,1)S(1)}, u32[]{:S(2)}, u32[]{:S(2)}) %all-to-all-start.2) | async-done | bytes 1048608 | tf_op jit(solution)/shard_map/all_to_all | solution.py:54
  66.0 10.3 %pad_maximum_fusion = bf16[6144,256]{1,0:T(8,128)(2,1)} fusion(bf16[2048,256]{1,0:T(8,128)(2,1)S(1)} %bitcast.47, bf16[1024,256]{1,0:T(8,128)(2,1)} %bitcast.5, bf16[3072,256]{1,0:T(8,128)(2,1)S(1)} %copy-done.6), kind=kLoop, calls=%fused_computation.43 | loop fusion | flops 9437184 | bytes 6291456 | tf_op jit(solution)/shard_map/concatenate | solution.py:56
  78.2 30.3 %while.20 = (s32[]{:T(128)}, f32[24,128,256]{2,0,1:T(8,128)}, s32[]{:T(128)}, s32[288]{0:T(512)S(1)}, s32[]{:T(128)}, /*index=5*/bf16[288,128,128]{2,1,0:T(8,128...) while((s32[]{:T(128)}, f32[24,128,256]{2,0,1:T(8,128)}, ...), condition=%wide.region_1.2_spmd, body=%wide.region_0.1_spmd.sunk | while | flops 1712068736 | bytes 78650992 | solution.py:82
  79.2 7.9 %gather_fusion = bf16[96,128,256]{2,1,0:T(8,128)(2,1)} fusion(bf16[48,128,256]{2,1,0:T(8,128)(2,1)} %get-tuple-element.264, s32[1024]{0:T(1024)S(1)} %pad_clamp_fusion.5), kind=kCustom, calls=%fused_computation.clone.1 | custom fusion | bytes 12583296 | tf_op jit(solution)/shard_map/while/body/gather | solution.py:73
  87.1 5.7 %fusion.61 = f32[96,128,256]{2,1,0:T(8,128)S(1)} fusion(bf16[96,128,256]{2,1,0:T(8,128)(2,1)} %gather_fusion, bf16[288,128,128]{2,1,0:T(8,128)(2,1)} %get-tuple-element.262, s32[]{:T(128)S(6)} %select_n.56), kind=kOutput, calls=%fused_computation.7.clone.1 | convolution fusion | flops 805306368 | bytes 22020100 | tf_op jit(solution)/shard_map/while/body/tij,tjd->tid/dot_general | solution.py:72
  92.8 13.7 %fusion.62 = f32[24,128,256]{2,0,1:T(8,128)S(1)} fusion(f32[24,128,256]{2,0,1:T(8,128)S(1)} %copy-done.4, f32[96,128,256]{2,1,0:T(8,128)S(1)} %fusion.61, f32[96]{0:T(128)S(1)} %compare_convert_fusion.4, s32[96]{0:T(128)S(1)} %dynamic_slice.32), kind=kOutput, calls=%fused_computation.9.clone.1 | convolution fusion | flops 906760704 | bytes 18875136 | tf_op jit(solution)/shard_map/while/body/tr,tid->rid/dot_general | solution.py:78
  115.5 2.9 fusion.31
  118.5 3.5 broadcast_in_dim.13
  121.9 30.3 %while.21 = (s32[]{:T(128)}, f32[48,128,256]{2,0,1:T(8,128)}, s32[]{:T(128)}, s32[288]{0:T(512)S(1)}, s32[]{:T(128)}, /*index=5*/bf16[288,128,128]{2,1,0:T(8,128...) while((s32[]{:T(128)}, f32[48,128,256]{2,0,1:T(8,128)}, ...), condition=%wide.region_3.4_spmd, body=%wide.region_2.3_spmd.sunk | while | flops 2618829312 | bytes 110108272 | solution.py:118
  122.9 5.9 %gather_fusion.1 = bf16[96,128,256]{2,1,0:T(8,128)(2,1)} fusion(bf16[24,128,256]{2,1,0:T(8,128)(2,1)S(1)} %get-tuple-element.300, s32[1024]{0:T(1024)S(1)} %pad_clamp_fusion.6), kind=kCustom, calls=%fused_computation.1.clone.1 | custom fusion | bytes 12583296 | tf_op jit(solution)/shard_map/while/body/gather | solution.py:109
  128.8 5.7 %fusion.67 = f32[96,128,256]{2,1,0:T(8,128)S(1)} fusion(bf16[96,128,256]{2,1,0:T(8,128)(2,1)} %gather_fusion.1, bf16[288,128,128]{2,1,0:T(8,128)(2,1)} %get-tuple-element.298, s32[]{:T(128)S(6)} %select_n.58), kind=kOutput, calls=%fused_computation.23.clone.1 | convolution fusion | flops 805306368 | bytes 22020100 | tf_op jit(solution)/shard_map/while/body/tji,tjd->tid/dot_general | solution.py:108
  134.6 14.8 %fusion.68 = f32[48,128,256]{2,0,1:T(8,128)S(1)} fusion(f32[48,128,256]{2,0,1:T(8,128)S(1)} %copy-done.2, f32[96,128,256]{2,1,0:T(8,128)S(1)} %fusion.67, f32[96]{0:T(128)S(1)} %compare_convert_fusion.5, s32[96]{0:T(128)S(1)} %dynamic_slice.35), kind=kOutput, calls=%fused_computation.25.clone.1 | convolution fusion | flops 1813521408 | bytes 25166592 | tf_op jit(solution)/shard_map/while/body/tc,tid->cid/dot_general | solution.py:114
  149.4 2.7 copy-done.3
  152.2 6.2 %copy.29 = bf16[48,128,256]{2,1,0:T(8,128)(2,1)S(1)} copy(f32[48,128,256]{2,0,1:T(8,128)} %get-tuple-element.90) | data formatting | bytes 9437184 | tf_op jit(solution)/shard_map/while | solution.py:118
  159.3 123.0 %all-to-all-start.3 = ((bf16[128,8,256]{2,1,0:T(8,128)(2,1)}), bf16[128,8,256]{2,1,0:T(8,128)(2,1)S(1)}, u32[]{:S(2)}, u32[]{:S(2)}) async-start(bf16[128,8,256]{2,1,0:T(8,128)(2,1)} %bitcast.15), calls=%async_computation.3 | async-start | bytes 1048576 | tf_op jit(solution)/shard_map/all_to_all | solution.py:131
  282.4 5.0 %fusion.34 = f32[256,256]{1,0:T(8,128)} fusion(f32[3072,256]{1,0:T(8,128)} %copy-done.7, f32[3072,256]{1,0:T(8,128)} %copy-done.15, bf16[3072,256]{1,0:T(8,128)(2,1)S(1)} %copy-done.11), kind=kOutput, calls=%fused_computation.52 | convolution fusion | flops 411303936 | bytes 8126464 | tf_op jit(solution)/shard_map/dot_general | solution.py:95
  289.6 2.6 copy.28
  292.2 139.4 %all-reduce.2.cloned.1.call-done = f32[256,256]{1,0:T(8,128)} async-done(((f32[256,256]{1,0:T(8,128)}), f32[256,256]{1,0:T(8,128)}) %all-reduce.2.cloned.1.call-update) | async-done | bytes 262160 | tf_op jit(solution)/shard_map/psum | solution.py:134
  433.3 9.7 %scatter_custom_fusion = f32[3072,256]{1,0:T(8,128)} fusion(f32[3072,256]{1,0:T(8,128)} %bitcast.48, s32[1024]{0:T(1024)} %bitcast.51, bf16[128,8,256]{2,1,0:T(8,128)(2,1)S(1)} %all-to-all-done.3), kind=kCustom, calls=%fused_computation.50 | custom fusion | flops 524288 | bytes 3670016 | tf_op jit(solution)/shard_map/scatter-add | solution.py:133
  (62 shorter events, 22.7 us)
Async XLA Ops:
  7.2 27.2 %copy-start = (bf16[3072,256]{1,0:T(8,128)(2,1)S(1)}, bf16[3072,256]{1,0:T(8,128)(2,1)}, u32[]{:S(2)}) copy-start(bf16[3072,256]{1,0:T(8,128)(2,1)} %param.17) | copy-start | bytes 4718596
  8.6 14.5 %all-to-all-start.1 = ((s32[8,1,2]{2,1,0:T(1,128)}), s32[8,1,2]{2,1,0:T(1,128)S(1)}, u32[]{:S(2)}, u32[]{:S(2)}) async-start(s32[8,1,2]{2,1,0:T(1,128)} %copy.25), calls=%async_computation.1 | async-start | bytes 8192 | tf_op jit(solution)/shard_map/all_to_all | solution.py:51
  16.4 0.6 copy-start.9
  23.2 42.9 %copy-start.6 = (bf16[3072,256]{1,0:T(8,128)(2,1)S(1)}, bf16[3072,256]{1,0:T(8,128)(2,1)}, u32[]{:S(2)}) copy-start(bf16[3072,256]{1,0:T(8,128)(2,1)} %param.15) | copy-start | bytes 4718596
  23.2 22.9 %all-to-all-start = ((bf16[128,8,256]{2,1,0:T(8,128)(2,1)}), bf16[128,8,256]{2,1,0:T(8,128)(2,1)}, u32[]{:S(2)}, u32[]{:S(2)}) async-start(bf16[128,8,256]{2,1,0:T(8,128)(2,1)} %bitcast.49), calls=%async_computation | async-start | bytes 1048576 | tf_op jit(solution)/shard_map/all_to_all | solution.py:49
  46.1 19.9 %all-to-all-start.2 = ((bf16[8,256,256]{2,1,0:T(8,128)(2,1)}), bf16[8,256,256]{2,1,0:T(8,128)(2,1)S(1)}, u32[]{:S(2)}, u32[]{:S(2)}) async-start(bf16[8,256,256]{2,1,0:T(8,128)(2,1)} %bitcast.46), calls=%async_computation.2 | async-start | bytes 2097152 | tf_op jit(solution)/shard_map/all_to_all | solution.py:54
  76.3 1.9 copy-start.13
  76.3 1.9 copy-start.14
  87.1 5.7 %copy-start.4 = (f32[24,128,256]{2,0,1:T(8,128)S(1)}, f32[24,128,256]{2,0,1:T(8,128)}, u32[]{:S(2)}) copy-start(f32[24,128,256]{2,0,1:T(8,128)} %get-tuple-element.246) | copy-start | bytes 9437188 | tf_op jit(solution)/shard_map/while
  106.4 1.7 copy-start.5
  110.7 1.4 copy-start.8
  112.1 0.9 copy-start.12
  113.0 2.3 copy-start.7
  113.0 2.5 copy-start.10
  115.3 3.2 copy-start.15
  128.8 5.7 %copy-start.2 = (f32[48,128,256]{2,0,1:T(8,128)S(1)}, f32[48,128,256]{2,0,1:T(8,128)}, u32[]{:S(2)}) copy-start(f32[48,128,256]{2,0,1:T(8,128)} %get-tuple-element.282) | copy-start | bytes 18874372 | tf_op jit(solution)/shard_map/while
  149.3 2.7 copy-start.3
  152.2 130.2 %copy-start.11 = (bf16[3072,256]{1,0:T(8,128)(2,1)S(1)}, bf16[3072,256]{1,0:T(8,128)(2,1)}, u32[]{:S(2)}) copy-start(bf16[3072,256]{1,0:T(8,128)(2,1)} %param.18) | copy-start | bytes 4718596
  159.3 274.0 %all-to-all-start.3 = ((bf16[128,8,256]{2,1,0:T(8,128)(2,1)}), bf16[128,8,256]{2,1,0:T(8,128)(2,1)S(1)}, u32[]{:S(2)}, u32[]{:S(2)}) async-start(bf16[128,8,256]{2,1,0:T(8,128)(2,1)} %bitcast.15), calls=%async_computation.3 | async-start | bytes 1048576 | tf_op jit(solution)/shard_map/all_to_all | solution.py:131
  282.3 149.3 %all-reduce.2.cloned.1.call-start = ((), (), s32[]{:S(2)}) async-start(), calls=%async_computation.4 | async-start | bytes 524288 | tf_op jit(solution)/shard_map/psum | solution.py:134
  289.5 153.5 %copy-start.1 = (bf16[3072,256]{1,0:T(8,128)(2,1)S(1)}, bf16[3072,256]{1,0:T(8,128)(2,1)}, u32[]{:S(2)}) copy-start(bf16[3072,256]{1,0:T(8,128)(2,1)} %param.17) | copy-start | bytes 4718596
Sparse Core Ops, SparseCore 0:
  288.5 143.0 all-reduce.1
where the time goes:
time: 456 us; the launch traced here: 450 us
  waiting for transfers between devices  164 us (36%)
  starting transfers between devices  145 us (32%)
  matrix products  50.1 us (11%)
  local copies, waits for them, and re-layouts  48.9 us (11%)
  other arithmetic  26.4 us (6%)
  between operations  15.1 us (3%)
    psum x1, waiting for transfers between devices, per_device(): weight_total = lax.psum(weight_part, ('dom', 'grp'))  139 us
    all_to_all x1, starting transfers between devices, per_device(): lax.all_to_all(fresh_grads, ('dom', 'grp'), split_axis=0, concat_axis=0,...  123 us
    dot_general x1, matrix products, backward_turn(): jnp.einsum('tc,tid->cid', onto_mask, spread, precision=lax.Precision.HIGH...  14.8 us
    all_to_all x1, waiting for transfers between devices, per_device(): lax.all_to_all(served, 'dom', split_axis=0, concat_axis=0, tiled=True)  14.4 us
    dot_general x1, matrix products, forward_turn(): jnp.einsum('tr,tid->rid', placing, products, precision=lax.Precision.HIGH...  13.7 us
    concatenate x1, other arithmetic, per_device(): columns = jnp.concatenate([inputs, arrived, cached], axis=0)  10.3 us
    all_to_all x1, waiting for transfers between devices, per_device(): lax.all_to_all(outgoing, ('dom', 'grp'), split_axis=0, concat_axis=0, til...  10.1 us
    all_to_all x1, starting transfers between devices, per_device(): lax.all_to_all(outgoing, ('dom', 'grp'), split_axis=0, concat_axis=0, til...  9.95 us
  transfers between devices with their start and end apart: 5, of which 3 were waited for; matrix products, arithmetic and copies ran while one was open for 5% of the time, Pallas kernels for 0%

commit v1 on v0

v1 whole, which is shorter than its diff:
```python
import math

import jax
import jax.numpy as jnp
from jax import lax
from jax.experimental import pallas as pl
from jax.experimental.pallas import tpu as pltpu
from jax.sharding import PartitionSpec as P

alpha_res = 0.1
beta_map = 0.4

MESH = pl.DeviceIdType.MESH
bf16, f32, i32 = jnp.bfloat16, jnp.float32, jnp.int32

DOM, GRP = 8, 16
D, BLK = 256, 128
ROW_BLOCKS = 24
FRESH = 8
COLUMNS = 48
TILES = 288
NO_TILE = TILES
GRAD_COLUMNS = ROW_BLOCKS + FRESH
FORWARD_PAIRS = (TILES + ROW_BLOCKS) // 2
BACKWARD_PAIRS = (TILES - 16 + GRAD_COLUMNS) // 2
NO_SUM = FORWARD_PAIRS
FORWARD_UNROLL, BACKWARD_UNROLL, MIDDLE_UNROLL = 12, 19, 3
DROPPED = 200


def each(count, visit):
    def body(i, carry):
        visit(i)
        return carry

    lax.fori_loop(1, count, body, 0)


def iota(shape, axis):
    return lax.broadcasted_iota(i32, shape, axis)


def total(x, axis):
    return jnp.sum(x, axis=axis, keepdims=True)


def as_column(row):
    n = row.shape[1]
    return total(jnp.where(iota((n, n), 0) == iota((n, n), 1), row, 0), 1)


def as_row(column):
    n = column.shape[0]
    return total(jnp.where(iota((n, n), 0) == iota((n, n), 1), column, 0), 0)


def pair_up(keys, other, groups):
    key_col, other_col = as_column(keys), as_column(other)
    hit = key_col == iota((TILES, BLK), 1)
    count_row = total(jnp.where(hit, 1, 0), 0)
    count_col = total(jnp.where(iota((groups, TILES), 0) == keys, 1, 0), 1)

    def pairs(count):
        return (count + 1) >> 1

    pairs_row, pairs_col = pairs(count_row), pairs(count_col)
    by_row, by_col = iota((groups, BLK), 1), iota((groups, BLK), 0)
    start_row = total(jnp.where(by_col < by_row, pairs_col, 0), 0)
    start_col = total(jnp.where(by_row < by_col, pairs_row, 0), 1)
    before = (keys == key_col) & (iota((TILES, TILES), 1) < iota((TILES, TILES), 0))
    rank = total(jnp.where(before, 1, 0), 1)
    slot = 2 * total(jnp.where(hit, start_row, 0), 1) + rank
    slot = jnp.where(key_col < groups, slot, 9999)
    match = slot == iota((TILES, 384), 1)
    tile_at = total(jnp.where(match, iota((TILES, 384), 0) - NO_TILE, 0), 0) + NO_TILE
    other_at = total(jnp.where(match, other_col, 0), 0)
    first = (start_col == iota((groups, 384), 1)) & (count_col > 0)
    goes_on = 1 - total(jnp.where(first, 1, 0), 0)
    last = jnp.where(count_row > 0, start_row + pairs_row - 1, NO_SUM)
    last = jnp.concatenate([last, jnp.zeros((1, 256), i32)], axis=1)
    return [tile_at, other_at, goes_on, last]


def pair_lists(row_ref, col_ref, live_count, out):
    rows, cols = row_ref[...], col_ref[...]
    live = iota((1, TILES), 1) < live_count
    forward = pair_up(jnp.where(live, rows, DROPPED), cols, ROW_BLOCKS)
    backward = pair_up(jnp.where(live & (cols < GRAD_COLUMNS), cols, DROPPED), rows, GRAD_COLUMNS)
    for i, v in enumerate(forward + backward):
        out[i : i + 1, :] = v


def run_pairs(lists, base, steps, unroll, product, sums):
    def body(s, running):
        for u in range(unroll):
            q = s * unroll + u
            a, b = lists[base, 2 * q], lists[base, 2 * q + 1]
            x, y = lists[base + 1, 2 * q], lists[base + 1, 2 * q + 1]
            running = jnp.where(lists[base + 2, q] > 0, running, 0.0) + product(a, b, x, y)
            sums[q] = running
        return running

    lax.fori_loop(0, steps // unroll, body, jnp.zeros((BLK, D), f32))


def to_message(x):
    x = x.reshape(16, 8, D)
    return jnp.concatenate([x[:, :, :BLK], x[:, :, BLK:]], axis=1).astype(bf16)


def from_message(x):
    x = x.astype(f32)
    return jnp.concatenate([x[:, :8, :], x[:, 8:, :]], axis=2).reshape(BLK, D).astype(bf16)


def kernel(
    inputs, initial, history, upstream, weight, tile_vals, tile_row, tile_col, tile_count, send_rows, cache_ask,
    layer_out, grad_inputs, grad_weight,
    columns, initial_v, history_v, upstream_v, weight_v, tiles, row_v, col_v, send_v, ask_s,
    outgoing, transit, arrived, served, ask_out, wanted, wanted_s, lists_v, lists,
    sums, layer_v, back, send_row, fresh, turn_a, turn_b, returned, grads_v,
    weight_part, part_out, part_in, group_sum, dom_in, weight_sum,
    local, far,
):
    d, g = lax.axis_index("dom"), lax.axis_index("grp")

    def dom_peer(i):
        return lax.rem(d + i, DOM)

    def grp_peer(i):
        return lax.rem(g + i, GRP)

    def push(src, dst, at, device):
        pltpu.make_async_remote_copy(
            src, dst, far.at[at], far.at[at + 1], device_id=device, device_id_type=MESH
        ).start()

    def keep(src, dst, at):
        pltpu.make_async_copy(src, dst, far.at[at + 1]).start()

    def landed(ref, at):
        pltpu.make_async_copy(ref, ref, far.at[at + 1]).wait()

    def left(ref, at):
        pltpu.make_async_copy(ref, ref, far.at[at]).wait()

    def load(at, src, dst):
        copy = pltpu.make_async_copy(src, dst, local.at[at])
        copy.start()
        return copy

    own_columns = columns.at[pl.ds(0, ROW_BLOCKS)]
    got_send = load(0, send_rows, send_v)
    got_inputs = load(1, inputs, own_columns)
    got_ask = load(2, cache_ask, ask_s)
    got_history = load(3, history, history_v)
    got_row = load(4, tile_row, row_v)
    got_col = load(5, tile_col, col_v)
    got_tiles = load(6, tile_vals, tiles.at[pl.ds(0, TILES)])
    got_initial = load(7, initial, initial_v)
    got_upstream = load(8, upstream, upstream_v)
    got_weight = load(9, weight, weight_v)

    barrier = pltpu.get_barrier_semaphore()
    each(DOM, lambda i: pl.semaphore_signal(barrier, inc=1, device_id=(dom_peer(i), g), device_id_type=MESH))
    each(GRP, lambda i: pl.semaphore_signal(barrier, inc=1, device_id=(d, grp_peer(i)), device_id_type=MESH))

    got_ask.wait()
    lane = lax.broadcasted_iota(i32, (8, BLK), 1)
    for e in range(DOM):
        ask_out[e] = jnp.where(lane == 0, ask_s[e, 0], ask_s[e, 1])

    got_send.wait()
    got_inputs.wait()

    def gather_rows(b, carry):
        listed = send_v[pl.ds(pl.multiple_of(b * 16, 16), 16), :]
        lanes, places = iota((16, 8, 8), 2), iota((16, 8, 8), 1)
        spread = jnp.broadcast_to(listed[:, None, :], (16, 8, 8))
        wanted_row = total(jnp.where(lanes == places, spread, 0), 2).reshape(BLK, 1)
        send_row[pl.ds(b, 1), :] = as_row(wanted_row)
        found = jnp.zeros((BLK, D), f32)
        for h in range(3):
            numbers = lax.broadcasted_iota(i32, (BLK, 1024), 1) + h * 1024
            pick = jnp.where(numbers == wanted_row, 1.0, 0.0).astype(bf16)
            block = columns[8 * h : 8 * h + 8].reshape(1024, D)
            found = found + jnp.dot(pick, block, preferred_element_type=f32)
        outgoing[b] = to_message(found)
        return carry

    lax.fori_loop(0, DOM, gather_rows, 0)
    pl.semaphore_wait(barrier, DOM + GRP - 2)

    each(DOM, lambda i: push(ask_out.at[dom_peer(i)], wanted.at[d], 0, (dom_peer(i), g)))
    keep(ask_out.at[d], wanted.at[d], 0)
    each(DOM, lambda i: push(outgoing.at[dom_peer(i)], transit.at[d], 2, (dom_peer(i), g)))
    keep(outgoing.at[d], transit.at[d], 2)

    got_history.wait()
    landed(wanted, 0)
    copy = pltpu.make_async_copy(wanted, wanted_s, local.at[0])
    copy.start()
    copy.wait()
    cached = columns.at[pl.ds(GRAD_COLUMNS + 2 * d, 2)]

    def serve(t):
        for j in range(2):
            served[t, j] = history_v[wanted_s[t, 0, j]]

    def ship(i):
        t = dom_peer(i)
        serve(t)
        push(served.at[t], cached, 4, (t, g))

    each(DOM, ship)
    serve(d)
    keep(served.at[d], cached, 4)

    landed(transit, 2)
    each(GRP, lambda i: push(transit.at[:, grp_peer(i)], arrived.at[:, g], 6, (d, grp_peer(i))))
    keep(transit.at[:, g], arrived.at[:, g], 6)

    got_row.wait()
    got_col.wait()
    pair_lists(row_v, col_v, tile_count[0], lists_v)
    copy = pltpu.make_async_copy(lists_v, lists, local.at[0])
    copy.start()
    tiles[NO_TILE] = jnp.zeros((BLK, BLK), bf16)
    sums[NO_SUM] = jnp.zeros((BLK, D), f32)
    copy.wait()
    got_initial.wait()
    got_upstream.wait()
    got_weight.wait()
    got_tiles.wait()

    landed(arrived, 6)
    for b in range(FRESH):
        columns[ROW_BLOCKS + b] = from_message(arrived[b])
    landed(columns.at[pl.ds(GRAD_COLUMNS, 16)], 4)

    def gather_product(a, b, x, y):
        left_side = jnp.concatenate([tiles[a], tiles[b]], axis=1)
        right_side = jnp.concatenate([columns[x], columns[y]], axis=0)
        return jnp.dot(left_side, right_side, preferred_element_type=f32)

    run_pairs(lists, 0, FORWARD_PAIRS, FORWARD_UNROLL, gather_product, sums)

    weight_part[...] = jnp.zeros_like(weight_part)

    def middle(r, carry):
        mixture = (1.0 - alpha_res) * sums[lists[3, r]] + alpha_res * initial_v[r].astype(f32)
        mixed_b = mixture.astype(bf16)
        w = weight_v[...]
        pre_act = (1.0 - beta_map) * mixture + beta_map * jnp.dot(mixed_b, w, preferred_element_type=f32)
        squash = 1.0 / (1.0 + jnp.exp(-pre_act))
        layer_v[r] = (pre_act * squash).astype(bf16)
        act_slope = upstream_v[r].astype(f32) * (squash * (1.0 + pre_act * (1.0 - squash)))
        slope_b = act_slope.astype(bf16)
        weight_part[...] += lax.dot_general(
            mixed_b, slope_b, (((0,), (0,)), ((), ())), preferred_element_type=f32
        )
        through = lax.dot_general(slope_b, w, (((1,), (1,)), ((), ())), preferred_element_type=f32)
        back[r] = ((1.0 - alpha_res) * ((1.0 - beta_map) * act_slope + beta_map * through)).astype(bf16)
        return carry

    lax.fori_loop(0, ROW_BLOCKS, middle, 0, unroll=MIDDLE_UNROLL)
    put_layer = load(0, layer_v, layer_out)

    part_out[...] = weight_part[...].reshape(GRP, 16, D)
    each(GRP, lambda i: push(part_out.at[grp_peer(i)], part_in.at[g], 8, (d, grp_peer(i))))
    keep(part_out.at[g], part_in.at[g], 8)

    def spread_product(a, b, x, y):
        left_side = jnp.concatenate([tiles[a], tiles[b]], axis=0)
        right_side = jnp.concatenate([back[x], back[y]], axis=0)
        return lax.dot_general(left_side, right_side, (((0,), (0,)), ((), ())), preferred_element_type=f32)

    run_pairs(lists, 4, BACKWARD_PAIRS, BACKWARD_UNROLL, spread_product, sums)

    for b in range(FRESH):
        fresh[b] = to_message(sums[lists[7, ROW_BLOCKS + b]]).reshape(8, 2, 16, BLK)
    parity, half = lax.rem(g, 2), g // 2
    other = 1 - parity

    def half_peer(i):
        return lax.rem(half + i, 8)

    each(DOM, lambda i: push(fresh.at[dom_peer(i), :, parity], turn_a.at[d], 10, (dom_peer(i), g)))
    keep(fresh.at[d, :, parity], turn_a.at[d], 10)

    def over_grp(i, carry):
        t = half_peer(i)
        push(fresh.at[:, t, other], turn_b.at[half], 12, (d, 2 * t + other))
        return carry

    lax.fori_loop(0, 8, over_grp, 0)

    landed(part_in, 8)
    group_sum[...] = jnp.sum(part_in[...], axis=0)
    each(DOM, lambda i: push(group_sum, dom_in.at[d], 14, (dom_peer(i), g)))
    keep(group_sum, dom_in.at[d], 14)

    landed(turn_a, 10)
    home = returned.at[:, half, parity]
    each(8, lambda i: push(turn_a.at[:, half_peer(i)], home, 16, (d, 2 * half_peer(i) + parity)))
    keep(turn_a.at[:, half], home, 16)
    landed(turn_b, 12)
    home = returned.at[d, :, other]
    each(DOM, lambda i: push(turn_b.at[:, dom_peer(i)], home, 18, (dom_peer(i), g)))
    pltpu.make_async_copy(turn_b.at[:, d], home, far.at[19]).start()

    landed(dom_in, 14)
    weight_sum[...] = jnp.sum(dom_in[...], axis=0) * (beta_map / math.sqrt(ROW_BLOCKS * BLK * DOM * GRP))
    each(GRP, lambda i: push(weight_sum, grad_weight.at[g], 20, (d, grp_peer(i))))
    keep(weight_sum, grad_weight.at[g], 20)

    landed(turn_a, 16)
    landed(turn_a, 18)
    rows_home = [from_message(returned[b].reshape(16, 16, BLK)) for b in range(8)]
    rows_home = jnp.concatenate(rows_home, axis=0)
    listed = jnp.concatenate([send_row[b : b + 1, :] for b in range(8)], axis=1)

    def finish(r, carry):
        numbers = lax.broadcasted_iota(i32, (BLK, 1024), 0) + r * BLK
        place = jnp.where(numbers == listed, 1.0, 0.0).astype(bf16)
        grads_v[r] = sums[lists[7, r]] + jnp.dot(place, rows_home, preferred_element_type=f32)
        return carry

    lax.fori_loop(0, ROW_BLOCKS, finish, 0, unroll=2)
    put_grads = load(1, grads_v, grad_inputs)

    left(ask_out.at[pl.ds(0, DOM - 1)], 0)
    left(outgoing.at[pl.ds(0, DOM - 1)], 2)
    left(served.at[pl.ds(0, DOM - 1)], 4)
    left(transit.at[:, pl.ds(0, GRP - 1)], 6)
    left(part_out.at[pl.ds(0, GRP - 1)], 8)
    left(turn_a.at[pl.ds(0, DOM - 1)], 10)
    left(turn_b, 12)
    left(dom_in.at[pl.ds(0, DOM - 1)], 14)
    left(turn_a.at[pl.ds(0, 7)], 16)
    left(turn_b.at[pl.ds(0, 7)], 18)
    left(part_in.at[pl.ds(0, GRP - 1)], 20)
    landed(grad_weight, 20)
    put_layer.wait()
    put_grads.wait()


def per_device(
    inputs, initial, history, upstream, weight, tile_vals, tile_row, tile_col, tile_count, send_rows, cache_ask
):
    hbm = pl.BlockSpec(memory_space=pl.ANY)
    vmem, smem, dma = pltpu.VMEM, pltpu.SMEM, pltpu.SemaphoreType.DMA
    blocks = (ROW_BLOCKS, BLK, D)
    shape = jax.ShapeDtypeStruct
    layer_out, grad_inputs, grad_weight = pl.pallas_call(
        kernel,
        out_shape=(shape(blocks, bf16), shape(blocks, f32), shape((GRP, 16, D), f32)),
        in_specs=[hbm] * 8 + [pl.BlockSpec(memory_space=smem)] + [hbm] * 2,
        out_specs=(hbm,) * 3,
        scratch_shapes=[
            vmem((COLUMNS, BLK, D), bf16),
            vmem(blocks, bf16),
            vmem(blocks, bf16),
            vmem(blocks, bf16),
            vmem((D, D), bf16),
            vmem((TILES + 1, BLK, BLK), bf16),
            vmem((1, TILES), i32),
            vmem((1, TILES), i32),
            vmem((128, 8), i32),
            smem((DOM, 2), i32),
            vmem((DOM, GRP, 16, BLK), bf16),
            vmem((DOM, GRP, 16, BLK), bf16),
            vmem((DOM, GRP, 16, BLK), bf16),
            vmem((DOM, 2, BLK, D), bf16),
            vmem((DOM, 8, BLK), i32),
            vmem((DOM, 8, BLK), i32),
            smem((DOM, 8, BLK), i32),
            vmem((8, 384), i32),
            smem((8, 384), i32),
            vmem((FORWARD_PAIRS + 1, BLK, D), f32),
            vmem(blocks, bf16),
            vmem(blocks, bf16),
            vmem((8, BLK), i32),
            vmem((DOM, 8, 2, 16, BLK), bf16),
            vmem((DOM, 8, 16, BLK), bf16),
            vmem((8, DOM, 16, BLK), bf16),
            vmem((DOM, 8, 2, 16, BLK), bf16),
            vmem(blocks, f32),
            vmem((D, D), f32),
            vmem((GRP, 16, D), f32),
            vmem((GRP, 16, D), f32),
            vmem((16, D), f32),
            vmem((DOM, 16, D), f32),
            vmem((16, D), f32),
            dma((10,)),
            dma((22,)),
        ],
        compiler_params=pltpu.CompilerParams(
            collective_id=0, has_side_effects=True, vmem_limit_bytes=60 * 1024 * 1024
        ),
    )(
        inputs.reshape(blocks),
        initial.reshape(blocks),
        history.reshape(blocks),
        upstream.reshape(blocks),
        weight,
        tile_vals,
        tile_row.reshape(1, TILES),
        tile_col.reshape(1, TILES),
        tile_count,
        send_rows.reshape(128, 8),
        cache_ask.reshape(DOM, 2),
    )
    rows = ROW_BLOCKS * BLK
    return layer_out.reshape(rows, D), grad_inputs.reshape(rows, D), grad_weight.reshape(D, D)


def solution(mesh):
    placed = (
        P(("dom", "grp"), None),
        P(("dom", "grp"), None),
        P(("dom", "grp"), None),
        P(("dom", "grp"), None),
        P(),
        P(("dom", "grp"), None, None),
        P(("dom", "grp")),
        P(("dom", "grp")),
        P(("dom", "grp")),
        P("dom", "grp", None, None),
        P("dom", "grp", None, None),
    )
    return jax.shard_map(
        per_device,
        mesh=mesh,
        in_specs=placed,
        out_specs=(P(("dom", "grp"), None), P(("dom", "grp"), None), P()),
        check_vma=False,
    )
```

time: 456 us -> 74.4 us (0.16); the launches traced: 450 us -> 74.1 us
  waiting for transfers between devices: 164 us -> 0 us
  starting transfers between devices: 145 us -> 0 us
  Pallas kernels: 0 us -> 62.4 us
  matrix products: 50.1 us -> 0 us
  local copies, waits for them, and re-layouts: 48.9 us -> 10.5 us
  other arithmetic: 26.4 us -> 0 us
  between operations: 15.1 us -> 1.3 us
    all_to_all x4 -> x0, starting transfers between devices: 145 us -> none  [the longest x1 123 us: per_device(): lax.all_to_all(fresh_grads, ('dom', 'grp'), split_axis=0, concat_axis=0,...]
    psum x1 -> x0, waiting for transfers between devices: 139 us -> none  [per_device(): weight_total = lax.psum(weight_part, ('dom', 'grp'))]
    pallas_call x0 -> x1, Pallas kernels: none -> 62.4 us  [per_device(): pl.pallas_call(kernel, out_shape=(shape(blocks, bf16), shape(blocks, f32)...]
    dot_general x7 -> x0, matrix products: 50.1 us -> none  [the longest x1 14.8 us: backward_turn(): jnp.einsum('tc,tid->cid', onto_mask, spread, precision=lax.Precision.HIGH...]
    all_to_all x4 -> x0, waiting for transfers between devices: 24.6 us -> none  [the longest x1 14.4 us: per_device(): lax.all_to_all(served, 'dom', split_axis=0, concat_axis=0, tiled=True)]
    gather x4 -> x0, local copies, waits for them, and re-layouts: 21.6 us -> none  [the longest x1 7.89 us: forward_turn(): col_blocks[col_pick]]
    while x9 -> x0, local copies, waits for them, and re-layouts: 10.6 us -> none  [the longest x1 6.24 us: per_device(): lax.fori_loop(0, turn_count, backward_turn, jnp.zeros((column_total, bloc...]
    concatenate x1 -> x0, other arithmetic: 10.3 us -> none  [per_device(): columns = jnp.concatenate([inputs, arrived, cached], axis=0)]
  transfers between devices with their start and end apart: 5 -> 0, of which waited for: 3 -> 0; matrix products, arithmetic and copies ran while one was open for 5% -> 0% of each run, Pallas kernels for 0% -> 0%
where the time goes in v1:
time: 74.4 us; the launch traced here: 74.1 us
  Pallas kernels  62.4 us (84%)
  local copies, waits for them, and re-layouts  10.5 us (14%)
  between operations  1.3 us (2%)
    pallas_call x1, Pallas kernels, per_device(): pl.pallas_call(kernel, out_shape=(shape(blocks, bf16), shape(blocks, f32)...  62.4 us
    unnamed x8, local copies, waits for them, and re-layouts  6.59 us

profile of v1, /device:TPU:1, one launch (start us, length us, event | category | flops | bytes accessed | tf_op | source)
XLA Modules:
  0.0 74.1 jit_solution(1758413069165324911)
XLA Ops:
  1.3 1.2 %reshape.43.tile_row = s32[1,288]{1,0:T(1,128)} reshape(s32[288]{0:T(512)} %param.17) | data formatting | bytes 2304 | tf_op jit(solution)/shard_map/reshape | solution.py:408
  2.5 1.3 %reshape.44.tile_col = s32[1,288]{1,0:T(1,128)} reshape(s32[288]{0:T(512)} %param.18) | data formatting | bytes 2304 | tf_op jit(solution)/shard_map/reshape | solution.py:409
  3.8 1.3 %copy.15.cache_ask = s32[8,2]{1,0:T(8,128)} copy(s32[8,2]{0,1:T(2,128)} %bitcast.17) | data formatting | bytes 128 | tf_op jit(solution)/shard_map/reshape | solution.py:412
  5.1 1.4 %copy.14 = s32[1,1,128,8]{3,2,1,0:T(8,128)} copy(s32[1,1,128,8]{2,3,1,0:T(8,128)} %param.20) | data formatting | bytes 8192 | tf_op args[9]
  6.6 62.4 %shard_map.130 = (bf16[24,128,256]{2,1,0:T(8,128)(2,1)}, f32[24,128,256]{2,1,0:T(8,128)}, f32[16,16,256]{2,1,0:T(8,128)}) custom-call(bf16[24,128,256]{2,1,0:T(8,128)(2,1)} %bitcast.10, bf16[24,128,256]{2,1,0:T(8,128)(2,1)} %bitcast.11, bf16[24,128,256]{2,1,0:T(8,128)(2,1)} %bitcast.12, bf16[24,128,256]{2,1,0:T(8,128)(2,1)} %bitcast.13, ...), custom_call_target="tpu_custom_call" | custom-call | tf_op jit(solution)/shard_map/pallas_call | solution.py:355
  68.9 0.0 copy-start
  69.0 2.8 %copy.20 = bf16[3072,256]{1,0:T(8,128)(2,1)} copy(bf16[3072,256]{1,0:T(8,128)(2,1)} %bitcast.14) | data formatting | bytes 3145728
  71.8 0.0 copy-done
  71.8 0.0 copy-start.1
  71.8 1.7 %copy.21 = f32[3072,256]{1,0:T(8,128)} copy(f32[3072,256]{1,0:T(8,128)S(1)} %bitcast.9) | data formatting | bytes 6291456
  73.4 0.0 copy-done.1
  73.4 0.7 copy.22
Async XLA Ops:
  68.9 2.8 %copy-start = (f32[24,128,256]{2,1,0:T(8,128)S(1)}, f32[24,128,256]{2,1,0:T(8,128)}, u32[]{:S(2)}) copy-start(f32[24,128,256]{2,1,0:T(8,128)} %get-tuple-element.7) | copy-start | bytes 9437188
  71.8 1.7 %copy-start.1 = (f32[16,16,256]{2,1,0:T(8,128)S(1)}, f32[16,16,256]{2,1,0:T(8,128)}, u32[]{:S(2)}) copy-start(f32[16,16,256]{2,1,0:T(8,128)} %get-tuple-element.8) | copy-start | bytes 786436

commit v2 on v1

--- a/solution.py
+++ b/solution.py
@@ -24,16 +24,18 @@
 FORWARD_PAIRS = (TILES + ROW_BLOCKS) // 2
 BACKWARD_PAIRS = (TILES - 16 + GRAD_COLUMNS) // 2
 NO_SUM = FORWARD_PAIRS
-FORWARD_UNROLL, BACKWARD_UNROLL, MIDDLE_UNROLL = 12, 19, 3
+FORWARD_UNROLL, BACKWARD_UNROLL = 78, 76
+MIDDLE_BLOCKS = 8
+FINISH_BLOCKS = 4
 DROPPED = 200
 
 
-def each(count, visit):
+def each(count, visit, first=1):
     def body(i, carry):
         visit(i)
         return carry
 
-    lax.fori_loop(1, count, body, 0)
+    lax.fori_loop(first, count, body, 0)
 
 
 def iota(shape, axis):
@@ -82,7 +84,7 @@
 
 
 def pair_lists(row_ref, col_ref, live_count, out):
-    rows, cols = row_ref[...], col_ref[...]
+    rows, cols = row_ref[...].reshape(1, TILES), col_ref[...].reshape(1, TILES)
     live = iota((1, TILES), 1) < live_count
     forward = pair_up(jnp.where(live, rows, DROPPED), cols, ROW_BLOCKS)
     backward = pair_up(jnp.where(live & (cols < GRAD_COLUMNS), cols, DROPPED), rows, GRAD_COLUMNS)
@@ -103,6 +105,12 @@
     lax.fori_loop(0, steps // unroll, body, jnp.zeros((BLK, D), f32))
 
 
+def listed_rows(listed, group):
+    shape = (16, 8, BLK)
+    spread = jnp.broadcast_to(listed[None], shape)
+    return total(jnp.where(iota(shape, 2) == iota(shape, 0) + group * 16, spread, 0), 2).reshape(BLK, 1)
+
+
 def to_message(x):
     x = x.reshape(16, 8, D)
     return jnp.concatenate([x[:, :, :BLK], x[:, :, BLK:]], axis=1).astype(bf16)
@@ -115,10 +123,10 @@
 
 def kernel(
     inputs, initial, history, upstream, weight, tile_vals, tile_row, tile_col, tile_count, send_rows, cache_ask,
-    layer_out, grad_inputs, grad_weight,
-    columns, initial_v, history_v, upstream_v, weight_v, tiles, row_v, col_v, send_v, ask_s,
+    layer_out, own_grads, returned, grad_weight,
+    columns, initial_v, history_v, upstream_v, weight_v, tiles, row_v, col_v, count_s, send_v, ask_s,
     outgoing, transit, arrived, served, ask_out, wanted, wanted_s, lists_v, lists,
-    sums, layer_v, back, send_row, fresh, turn_a, turn_b, returned, grads_v,
+    sums, layer_v, back, fresh, turn_a, turn_b, grads_v,
     weight_part, part_out, part_in, group_sum, dom_in, weight_sum,
     local, far,
 ):
@@ -149,9 +157,12 @@
         copy.start()
         return copy
 
-    own_columns = columns.at[pl.ds(0, ROW_BLOCKS)]
+    barrier = pltpu.get_barrier_semaphore()
+    each(DOM, lambda i: pl.semaphore_signal(barrier, inc=1, device_id=(dom_peer(i), g), device_id_type=MESH))
+    each(GRP, lambda i: pl.semaphore_signal(barrier, inc=1, device_id=(d, grp_peer(i)), device_id_type=MESH))
+
     got_send = load(0, send_rows, send_v)
-    got_inputs = load(1, inputs, own_columns)
+    got_inputs = load(1, inputs, columns.at[pl.ds(0, ROW_BLOCKS)])
     got_ask = load(2, cache_ask, ask_s)
     got_history = load(3, history, history_v)
     got_row = load(4, tile_row, row_v)
@@ -160,40 +171,41 @@
     got_initial = load(7, initial, initial_v)
     got_upstream = load(8, upstream, upstream_v)
     got_weight = load(9, weight, weight_v)
-
-    barrier = pltpu.get_barrier_semaphore()
-    each(DOM, lambda i: pl.semaphore_signal(barrier, inc=1, device_id=(dom_peer(i), g), device_id_type=MESH))
-    each(GRP, lambda i: pl.semaphore_signal(barrier, inc=1, device_id=(d, grp_peer(i)), device_id_type=MESH))
+    got_count = load(10, tile_count, count_s)
 
     got_ask.wait()
-    lane = lax.broadcasted_iota(i32, (8, BLK), 1)
+    lane = iota((8, BLK), 1)
     for e in range(DOM):
-        ask_out[e] = jnp.where(lane == 0, ask_s[e, 0], ask_s[e, 1])
+        ask_out[e] = jnp.where(lane == 0, ask_s[0, e], ask_s[1, e])
 
     got_send.wait()
     got_inputs.wait()
 
-    def gather_rows(b, carry):
-        listed = send_v[pl.ds(pl.multiple_of(b * 16, 16), 16), :]
-        lanes, places = iota((16, 8, 8), 2), iota((16, 8, 8), 1)
-        spread = jnp.broadcast_to(listed[:, None, :], (16, 8, 8))
-        wanted_row = total(jnp.where(lanes == places, spread, 0), 2).reshape(BLK, 1)
-        send_row[pl.ds(b, 1), :] = as_row(wanted_row)
+    def gather_rows(i):
+        t = dom_peer(i)
+        wanted_row = listed_rows(send_v[...], t)
         found = jnp.zeros((BLK, D), f32)
         for h in range(3):
-            numbers = lax.broadcasted_iota(i32, (BLK, 1024), 1) + h * 1024
-            pick = jnp.where(numbers == wanted_row, 1.0, 0.0).astype(bf16)
+            pick = jnp.where(iota((BLK, 1024), 1) + h * 1024 == wanted_row, 1.0, 0.0).astype(bf16)
             block = columns[8 * h : 8 * h + 8].reshape(1024, D)
             found = found + jnp.dot(pick, block, preferred_element_type=f32)
-        outgoing[b] = to_message(found)
-        return carry
-
-    lax.fori_loop(0, DOM, gather_rows, 0)
+        outgoing[t] = to_message(found)
+
+    def push_rows(i):
+        push(outgoing.at[dom_peer(i)], transit.at[d], 2, (dom_peer(i), g))
+
+    def gather_and_push(i):
+        gather_rows(i)
+        push_rows(i)
+
+    early = 4
+    each(early, gather_rows)
     pl.semaphore_wait(barrier, DOM + GRP - 2)
-
     each(DOM, lambda i: push(ask_out.at[dom_peer(i)], wanted.at[d], 0, (dom_peer(i), g)))
     keep(ask_out.at[d], wanted.at[d], 0)
-    each(DOM, lambda i: push(outgoing.at[dom_peer(i)], transit.at[d], 2, (dom_peer(i), g)))
+    each(early, push_rows)
+    each(DOM, gather_and_push, early)
+    gather_rows(0)
     keep(outgoing.at[d], transit.at[d], 2)
 
     got_history.wait()
@@ -222,7 +234,8 @@
 
     got_row.wait()
     got_col.wait()
-    pair_lists(row_v, col_v, tile_count[0], lists_v)
+    got_count.wait()
+    pair_lists(row_v, col_v, count_s[0], lists_v)
     copy = pltpu.make_async_copy(lists_v, lists, local.at[0])
     copy.start()
     tiles[NO_TILE] = jnp.zeros((BLK, BLK), bf16)
@@ -248,22 +261,28 @@
     weight_part[...] = jnp.zeros_like(weight_part)
 
     def middle(r, carry):
-        mixture = (1.0 - alpha_res) * sums[lists[3, r]] + alpha_res * initial_v[r].astype(f32)
+        first = r * MIDDLE_BLOCKS
+        at = pl.ds(first, MIDDLE_BLOCKS)
+        rows, w = MIDDLE_BLOCKS * BLK, weight_v[...]
+        gathered = jnp.concatenate([sums[lists[3, first + i]] for i in range(MIDDLE_BLOCKS)], axis=0)
+        start = initial_v[at].reshape(rows, D).astype(f32)
+        mixture = (1.0 - alpha_res) * gathered + alpha_res * start
         mixed_b = mixture.astype(bf16)
-        w = weight_v[...]
         pre_act = (1.0 - beta_map) * mixture + beta_map * jnp.dot(mixed_b, w, preferred_element_type=f32)
         squash = 1.0 / (1.0 + jnp.exp(-pre_act))
-        layer_v[r] = (pre_act * squash).astype(bf16)
-        act_slope = upstream_v[r].astype(f32) * (squash * (1.0 + pre_act * (1.0 - squash)))
+        layer_v[at] = (pre_act * squash).astype(bf16).reshape(MIDDLE_BLOCKS, BLK, D)
+        above = upstream_v[at].reshape(rows, D).astype(f32)
+        act_slope = above * (squash * (1.0 + pre_act * (1.0 - squash)))
         slope_b = act_slope.astype(bf16)
         weight_part[...] += lax.dot_general(
             mixed_b, slope_b, (((0,), (0,)), ((), ())), preferred_element_type=f32
         )
         through = lax.dot_general(slope_b, w, (((1,), (1,)), ((), ())), preferred_element_type=f32)
-        back[r] = ((1.0 - alpha_res) * ((1.0 - beta_map) * act_slope + beta_map * through)).astype(bf16)
+        grad = (1.0 - alpha_res) * ((1.0 - beta_map) * act_slope + beta_map * through)
+        back[at] = grad.astype(bf16).reshape(MIDDLE_BLOCKS, BLK, D)
         return carry
 
-    lax.fori_loop(0, ROW_BLOCKS, middle, 0, unroll=MIDDLE_UNROLL)
+    lax.fori_loop(0, ROW_BLOCKS // MIDDLE_BLOCKS, middle, 0)
     put_layer = load(0, layer_v, layer_out)
 
     part_out[...] = weight_part[...].reshape(GRP, 16, D)
@@ -294,6 +313,13 @@
         return carry
 
     lax.fori_loop(0, 8, over_grp, 0)
+
+    def own(r, carry):
+        grads_v[r] = sums[lists[7, r]]
+        return carry
+
+    lax.fori_loop(0, ROW_BLOCKS, own, 0)
+    put_grads = load(1, grads_v, own_grads)
 
     landed(part_in, 8)
     group_sum[...] = jnp.sum(part_in[...], axis=0)
@@ -313,21 +339,6 @@
     weight_sum[...] = jnp.sum(dom_in[...], axis=0) * (beta_map / math.sqrt(ROW_BLOCKS * BLK * DOM * GRP))
     each(GRP, lambda i: push(weight_sum, grad_weight.at[g], 20, (d, grp_peer(i))))
     keep(weight_sum, grad_weight.at[g], 20)
-
-    landed(turn_a, 16)
-    landed(turn_a, 18)
-    rows_home = [from_message(returned[b].reshape(16, 16, BLK)) for b in range(8)]
-    rows_home = jnp.concatenate(rows_home, axis=0)
-    listed = jnp.concatenate([send_row[b : b + 1, :] for b in range(8)], axis=1)
-
-    def finish(r, carry):
-        numbers = lax.broadcasted_iota(i32, (BLK, 1024), 0) + r * BLK
-        place = jnp.where(numbers == listed, 1.0, 0.0).astype(bf16)
-        grads_v[r] = sums[lists[7, r]] + jnp.dot(place, rows_home, preferred_element_type=f32)
-        return carry
-
-    lax.fori_loop(0, ROW_BLOCKS, finish, 0, unroll=2)
-    put_grads = load(1, grads_v, grad_inputs)
 
     left(ask_out.at[pl.ds(0, DOM - 1)], 0)
     left(outgoing.at[pl.ds(0, DOM - 1)], 2)
@@ -340,9 +351,28 @@
     left(turn_a.at[pl.ds(0, 7)], 16)
     left(turn_b.at[pl.ds(0, 7)], 18)
     left(part_in.at[pl.ds(0, GRP - 1)], 20)
+    landed(turn_a, 16)
+    landed(turn_a, 18)
     landed(grad_weight, 20)
     put_layer.wait()
     put_grads.wait()
+
+
+def finish(send_rows, own, layer, weight_in, returned, grad_inputs, layer_out, grad_weight, rows_home, listed):
+    step = pl.program_id(0)
+
+    @pl.when(step == 0)
+    def _():
+        grad_weight[...] = weight_in[...]
+        for b in range(DOM):
+            rows_home[b * BLK : (b + 1) * BLK, :] = from_message(returned[b].reshape(16, 16, BLK))
+            listed[:, b * BLK : (b + 1) * BLK] = as_row(listed_rows(send_rows[...], b))
+
+    layer_out[...] = layer[...]
+    count = FINISH_BLOCKS * BLK
+    place = jnp.where(iota((count, 1024), 0) + step * count == listed[...], 1.0, 0.0).astype(bf16)
+    home = jnp.dot(place, rows_home[...], preferred_element_type=f32)
+    grad_inputs[...] = own[...] + home.reshape(FINISH_BLOCKS, BLK, D)
 
 
 def per_device(
@@ -352,11 +382,13 @@
     vmem, smem, dma = pltpu.VMEM, pltpu.SMEM, pltpu.SemaphoreType.DMA
     blocks = (ROW_BLOCKS, BLK, D)
     shape = jax.ShapeDtypeStruct
-    layer_out, grad_inputs, grad_weight = pl.pallas_call(
+    send_rows = jnp.swapaxes(send_rows.reshape(128, 8), 0, 1)
+    back_home = (DOM, 8, 2, 16, BLK)
+    layer_out, own_grads, returned, grad_weight = pl.pallas_call(
         kernel,
-        out_shape=(shape(blocks, bf16), shape(blocks, f32), shape((GRP, 16, D), f32)),
-        in_specs=[hbm] * 8 + [pl.BlockSpec(memory_space=smem)] + [hbm] * 2,
-        out_specs=(hbm,) * 3,
+        out_shape=(shape(blocks, bf16), shape(blocks, f32), shape(back_home, bf16), shape((GRP, 16, D), f32)),
+        in_specs=[hbm] * 11,
+        out_specs=(hbm,) * 4,
         scratch_shapes=[
             vmem((COLUMNS, BLK, D), bf16),
             vmem(blocks, bf16),
@@ -364,10 +396,11 @@
             vmem(blocks, bf16),
             vmem((D, D), bf16),
             vmem((TILES + 1, BLK, BLK), bf16),
-            vmem((1, TILES), i32),
-            vmem((1, TILES), i32),
-            vmem((128, 8), i32),
-            smem((DOM, 2), i32),
+            vmem((TILES,), i32),
+            vmem((TILES,), i32),
+            smem((1,), i32),
+            vmem((8, 128), i32),
+            smem((2, DOM), i32),
             vmem((DOM, GRP, 16, BLK), bf16),
             vmem((DOM, GRP, 16, BLK), bf16),
             vmem((DOM, GRP, 16, BLK), bf16),
@@ -380,11 +413,9 @@
             vmem((FORWARD_PAIRS + 1, BLK, D), f32),
             vmem(blocks, bf16),
             vmem(blocks, bf16),
-            vmem((8, BLK), i32),
             vmem((DOM, 8, 2, 16, BLK), bf16),
             vmem((DOM, 8, 16, BLK), bf16),
             vmem((8, DOM, 16, BLK), bf16),
-            vmem((DOM, 8, 2, 16, BLK), bf16),
             vmem(blocks, f32),
             vmem((D, D), f32),
             vmem((GRP, 16, D), f32),
@@ -392,7 +423,7 @@
             vmem((16, D), f32),
             vmem((DOM, 16, D), f32),
             vmem((16, D), f32),
-            dma((10,)),
+            dma((11,)),
             dma((22,)),
         ],
         compiler_params=pltpu.CompilerParams(
@@ -405,12 +436,23 @@
         upstream.reshape(blocks),
         weight,
         tile_vals,
-        tile_row.reshape(1, TILES),
-        tile_col.reshape(1, TILES),
+        tile_row,
+        tile_col,
         tile_count,
-        send_rows.reshape(128, 8),
-        cache_ask.reshape(DOM, 2),
+        send_rows,
+        jnp.swapaxes(cache_ask.reshape(DOM, 2), 0, 1),
     )
+    whole = pl.BlockSpec(memory_space=vmem)
+    part = pl.BlockSpec((FINISH_BLOCKS, BLK, D), lambda i: (i, 0, 0))
+    grad_inputs, layer_out, grad_weight = pl.pallas_call(
+        finish,
+        grid=(ROW_BLOCKS // FINISH_BLOCKS,),
+        out_shape=(shape(blocks, f32), shape(blocks, bf16), shape((GRP, 16, D), f32)),
+        in_specs=[whole, part, part, whole, whole],
+        out_specs=(part, part, whole),
+        scratch_shapes=[vmem((1024, D), bf16), vmem((1, 1024), i32)],
+        compiler_params=pltpu.CompilerParams(vmem_limit_bytes=60 * 1024 * 1024),
+    )(send_rows, own_grads, layer_out, grad_weight, returned)
     rows = ROW_BLOCKS * BLK
     return layer_out.reshape(rows, D), grad_inputs.reshape(rows, D), grad_weight.reshape(D, D)
 

time: 74.4 us -> 60.6 us (0.81)
  local copies, waits for them, and re-layouts: 10.5 us -> 0 us
  Pallas kernels: 62.4 us -> 59.1 us
    pallas_call x1, Pallas kernels: 62.4 us -> 51.7 us  [per_device(): pl.pallas_call(kernel, out_shape=(shape(blocks, bf16), shape(blocks, f32)...]
    pallas_call x0 -> x1, Pallas kernels: none -> 7.35 us  [per_device(): pl.pallas_call(finish, grid=(ROW_BLOCKS // FINISH_BLOCKS,), out_shape=(sh...]
    unnamed x8 -> x0, local copies, waits for them, and re-layouts: 6.59 us -> none
    reshape x3 -> x0, local copies, waits for them, and re-layouts: 3.86 us -> none  [the longest x1 1.34 us: per_device(): cache_ask.reshape(DOM, 2)]
where the time goes in v2:
time: 60.6 us; the launch traced here: 60.4 us
  Pallas kernels  59.1 us (98%)
  between operations  1.29 us (2%)
    pallas_call x1, Pallas kernels, per_device(): pl.pallas_call(kernel, out_shape=(shape(blocks, bf16), shape(blocks, f32)...  51.7 us
    pallas_call x1, Pallas kernels, per_device(): pl.pallas_call(finish, grid=(ROW_BLOCKS // FINISH_BLOCKS,), out_shape=(sh...  7.35 us

profile of v2, /device:TPU:1, one launch (start us, length us, event | category | flops | bytes accessed | tf_op | source)
XLA Modules:
  0.0 60.4 jit_solution(16914749248541293352)
XLA Ops:
  1.3 51.7 %shard_map.130 = (bf16[24,128,256]{2,1,0:T(8,128)(2,1)}, f32[24,128,256]{2,1,0:T(8,128)}, bf16[8,8,2,16,128]{4,3,2,1,0:T(8,128)(2,1)}, f32[16,16,256]{2,1,0:T(8,128)}) custom-call(bf16[24,128,256]{2,1,0:T(8,128)(2,1)} %bitcast.13, bf16[24,128,256]{2,1,0:T(8,128)(2,1)} %bitcast.14, bf16[24,128,256]{2,1,0:T(8,128)(2,1)} %bitcast.15, ...), custom_call_target="tpu_custom_call" | custom-call | tf_op jit(solution)/shard_map/pallas_call | solution.py:387
  53.0 7.4 %shard_map.131 = (f32[24,128,256]{2,1,0:T(8,128)}, bf16[24,128,256]{2,1,0:T(8,128)(2,1)}, f32[16,16,256]{2,1,0:T(8,128)}) custom-call(s32[8,128]{1,0:T(8,128)} %bitcast.18, f32[24,128,256]{2,1,0:T(8,128)} %get-tuple-element.10.own, bf16[24,128,256]{2,1,0:T(8,128)(2,1)} %get-tuple-element.11.layer, f32[16,16,256]{2,1,0:T(8,128)} %get-tuple-element.12.weight_in, ...), custom_call_target="tpu_custom_call" | custom-call | tf_op jit(solution)/shard_map/pallas_call | solution.py:447

commit v3 on v2

--- a/solution.py
+++ b/solution.py
@@ -22,12 +22,14 @@
 NO_TILE = TILES
 GRAD_COLUMNS = ROW_BLOCKS + FRESH
 FORWARD_PAIRS = (TILES + ROW_BLOCKS) // 2
-BACKWARD_PAIRS = (TILES - 16 + GRAD_COLUMNS) // 2
+FRESH_PAIRS = (TILES - COLUMNS + 2 * FRESH) // 2
+OWN_PAIRS = (TILES - COLUMNS + 2 * ROW_BLOCKS) // 2
 NO_SUM = FORWARD_PAIRS
-FORWARD_UNROLL, BACKWARD_UNROLL = 78, 76
+FORWARD_UNROLL, FRESH_UNROLL, OWN_UNROLL = 78, 64, 72
 MIDDLE_BLOCKS = 8
-FINISH_BLOCKS = 4
+FINISH_BLOCKS = 12
 DROPPED = 200
+WEIGHT_SUM = f32
 
 
 def each(count, visit, first=1):
@@ -87,8 +89,10 @@
     rows, cols = row_ref[...].reshape(1, TILES), col_ref[...].reshape(1, TILES)
     live = iota((1, TILES), 1) < live_count
     forward = pair_up(jnp.where(live, rows, DROPPED), cols, ROW_BLOCKS)
-    backward = pair_up(jnp.where(live & (cols < GRAD_COLUMNS), cols, DROPPED), rows, GRAD_COLUMNS)
-    for i, v in enumerate(forward + backward):
+    arrived = live & (cols >= ROW_BLOCKS) & (cols < GRAD_COLUMNS)
+    fresh = pair_up(jnp.where(arrived, cols - ROW_BLOCKS, DROPPED), rows, FRESH)
+    own = pair_up(jnp.where(live & (cols < ROW_BLOCKS), cols, DROPPED), rows, ROW_BLOCKS)
+    for i, v in enumerate(forward + fresh + own):
         out[i : i + 1, :] = v
 
 
@@ -126,7 +130,7 @@
     layer_out, own_grads, returned, grad_weight,
     columns, initial_v, history_v, upstream_v, weight_v, tiles, row_v, col_v, count_s, send_v, ask_s,
     outgoing, transit, arrived, served, ask_out, wanted, wanted_s, lists_v, lists,
-    sums, layer_v, back, fresh, turn_a, turn_b, grads_v,
+    sums, layer_v, grads_v, back, fresh, turn_a, turn_b,
     weight_part, part_out, part_in, group_sum, dom_in, weight_sum,
     local, far,
 ):
@@ -164,6 +168,13 @@
     got_send = load(0, send_rows, send_v)
     got_inputs = load(1, inputs, columns.at[pl.ds(0, ROW_BLOCKS)])
     got_ask = load(2, cache_ask, ask_s)
+    got_ask.wait()
+    lane = iota((8, BLK), 1)
+    for e in range(DOM):
+        ask_out[e] = jnp.where(lane == 0, ask_s[0, e], ask_s[1, e])
+
+    got_send.wait()
+    got_inputs.wait()
     got_history = load(3, history, history_v)
     got_row = load(4, tile_row, row_v)
     got_col = load(5, tile_col, col_v)
@@ -172,14 +183,6 @@
     got_upstream = load(8, upstream, upstream_v)
     got_weight = load(9, weight, weight_v)
     got_count = load(10, tile_count, count_s)
-
-    got_ask.wait()
-    lane = iota((8, BLK), 1)
-    for e in range(DOM):
-        ask_out[e] = jnp.where(lane == 0, ask_s[0, e], ask_s[1, e])
-
-    got_send.wait()
-    got_inputs.wait()
 
     def gather_rows(i):
         t = dom_peer(i)
@@ -285,7 +288,7 @@
     lax.fori_loop(0, ROW_BLOCKS // MIDDLE_BLOCKS, middle, 0)
     put_layer = load(0, layer_v, layer_out)
 
-    part_out[...] = weight_part[...].reshape(GRP, 16, D)
+    part_out[...] = weight_part[...].astype(bf16).reshape(GRP, 16, D)
     each(GRP, lambda i: push(part_out.at[grp_peer(i)], part_in.at[g], 8, (d, grp_peer(i))))
     keep(part_out.at[g], part_in.at[g], 8)
 
@@ -294,10 +297,10 @@
         right_side = jnp.concatenate([back[x], back[y]], axis=0)
         return lax.dot_general(left_side, right_side, (((0,), (0,)), ((), ())), preferred_element_type=f32)
 
-    run_pairs(lists, 4, BACKWARD_PAIRS, BACKWARD_UNROLL, spread_product, sums)
+    run_pairs(lists, 4, FRESH_PAIRS, FRESH_UNROLL, spread_product, sums)
 
     for b in range(FRESH):
-        fresh[b] = to_message(sums[lists[7, ROW_BLOCKS + b]]).reshape(8, 2, 16, BLK)
+        fresh[b] = to_message(sums[lists[7, b]]).reshape(8, 2, 16, BLK)
     parity, half = lax.rem(g, 2), g // 2
     other = 1 - parity
 
@@ -314,17 +317,12 @@
 
     lax.fori_loop(0, 8, over_grp, 0)
 
-    def own(r, carry):
-        grads_v[r] = sums[lists[7, r]]
-        return carry
-
-    lax.fori_loop(0, ROW_BLOCKS, own, 0)
-    put_grads = load(1, grads_v, own_grads)
-
     landed(part_in, 8)
-    group_sum[...] = jnp.sum(part_in[...], axis=0)
+    group_sum[...] = jnp.sum(part_in[...].astype(f32), axis=0)
     each(DOM, lambda i: push(group_sum, dom_in.at[d], 14, (dom_peer(i), g)))
     keep(group_sum, dom_in.at[d], 14)
+
+    run_pairs(lists, 8, OWN_PAIRS, OWN_UNROLL, spread_product, sums)
 
     landed(turn_a, 10)
     home = returned.at[:, half, parity]
@@ -336,9 +334,17 @@
     pltpu.make_async_copy(turn_b.at[:, d], home, far.at[19]).start()
 
     landed(dom_in, 14)
-    weight_sum[...] = jnp.sum(dom_in[...], axis=0) * (beta_map / math.sqrt(ROW_BLOCKS * BLK * DOM * GRP))
+    whole_sum = jnp.sum(dom_in[...], axis=0)
+    weight_sum[...] = (whole_sum * (beta_map / math.sqrt(ROW_BLOCKS * BLK * DOM * GRP))).astype(WEIGHT_SUM)
     each(GRP, lambda i: push(weight_sum, grad_weight.at[g], 20, (d, grp_peer(i))))
     keep(weight_sum, grad_weight.at[g], 20)
+
+    def own(r, carry):
+        grads_v[r] = sums[lists[11, r]]
+        return carry
+
+    lax.fori_loop(0, ROW_BLOCKS, own, 0, unroll=4)
+    put_grads = load(1, grads_v, own_grads)
 
     left(ask_out.at[pl.ds(0, DOM - 1)], 0)
     left(outgoing.at[pl.ds(0, DOM - 1)], 2)
@@ -350,7 +356,7 @@
     left(dom_in.at[pl.ds(0, DOM - 1)], 14)
     left(turn_a.at[pl.ds(0, 7)], 16)
     left(turn_b.at[pl.ds(0, 7)], 18)
-    left(part_in.at[pl.ds(0, GRP - 1)], 20)
+    left(grad_weight.at[pl.ds(0, GRP - 1)], 20)
     landed(turn_a, 16)
     landed(turn_a, 18)
     landed(grad_weight, 20)
@@ -358,21 +364,53 @@
     put_grads.wait()
 
 
-def finish(send_rows, own, layer, weight_in, returned, grad_inputs, layer_out, grad_weight, rows_home, listed):
-    step = pl.program_id(0)
-
-    @pl.when(step == 0)
-    def _():
-        grad_weight[...] = weight_in[...]
-        for b in range(DOM):
-            rows_home[b * BLK : (b + 1) * BLK, :] = from_message(returned[b].reshape(16, 16, BLK))
-            listed[:, b * BLK : (b + 1) * BLK] = as_row(listed_rows(send_rows[...], b))
-
-    layer_out[...] = layer[...]
-    count = FINISH_BLOCKS * BLK
-    place = jnp.where(iota((count, 1024), 0) + step * count == listed[...], 1.0, 0.0).astype(bf16)
-    home = jnp.dot(place, rows_home[...], preferred_element_type=f32)
-    grad_inputs[...] = own[...] + home.reshape(FINISH_BLOCKS, BLK, D)
+def finish(
+    send_rows, own, layer, weight_in, returned, grad_inputs, layer_out, grad_weight,
+    send_v, own_v, layer_v, weight_v, returned_v, grads, weight_f, sems,
+):
+    parts = ROW_BLOCKS // FINISH_BLOCKS
+
+    def move(at, src, dst):
+        copy = pltpu.make_async_copy(src, dst, sems.at[at])
+        copy.start()
+        return copy
+
+    def blocks(ref, step):
+        return ref.at[pl.ds(step * FINISH_BLOCKS, FINISH_BLOCKS)]
+
+    got_send = move(0, send_rows, send_v)
+    got_returned = move(1, returned, returned_v)
+    got_own = [move(4 + step, blocks(own, step), blocks(own_v, step)) for step in range(parts)]
+    got_layer = move(2, layer, layer_v)
+    got_weight = move(3, weight_in, weight_v)
+
+    got_send.wait()
+    listed = jnp.concatenate([as_row(listed_rows(send_v[...], b)) for b in range(DOM)], axis=1)
+    got_returned.wait()
+    rows_home = jnp.concatenate([from_message(returned_v[b].reshape(16, 16, BLK)) for b in range(DOM)], axis=0)
+    block_of, row_of = listed >> 7, (listed & (BLK - 1)).astype(f32)
+    numbers = iota((BLK, 1024), 0).astype(bf16)
+    one, zero = jnp.ones((BLK, 1024), bf16), jnp.zeros((BLK, 1024), bf16)
+    puts = []
+    for step in range(parts):
+        home = []
+        for r in range(step * FINISH_BLOCKS, (step + 1) * FINISH_BLOCKS):
+            in_block = jnp.where(block_of == r, row_of, -1.0).astype(bf16)
+            place = jnp.where(numbers == in_block, one, zero)
+            home.append(jnp.dot(place, rows_home, preferred_element_type=f32)[None])
+        home = jnp.concatenate(home, axis=0)
+        got_own[step].wait()
+        at = pl.ds(step * FINISH_BLOCKS, FINISH_BLOCKS)
+        grads[at] = own_v[at] + home
+        puts.append(move(4 + step, blocks(grads, step), blocks(grad_inputs, step)))
+        if step == 0:
+            got_layer.wait()
+            puts.append(move(2, layer_v, layer_out))
+            got_weight.wait()
+            weight_f[...] = weight_v[...].astype(f32)
+            puts.append(move(3, weight_f, grad_weight))
+    for copy in puts:
+        copy.wait()
 
 
 def per_device(
@@ -386,7 +424,7 @@
     back_home = (DOM, 8, 2, 16, BLK)
     layer_out, own_grads, returned, grad_weight = pl.pallas_call(
         kernel,
-        out_shape=(shape(blocks, bf16), shape(blocks, f32), shape(back_home, bf16), shape((GRP, 16, D), f32)),
+        out_shape=(shape(blocks, bf16), shape(blocks, f32), shape(back_home, bf16), shape((GRP, 16, D), WEIGHT_SUM)),
         in_specs=[hbm] * 11,
         out_specs=(hbm,) * 4,
         scratch_shapes=[
@@ -408,21 +446,21 @@
             vmem((DOM, 8, BLK), i32),
             vmem((DOM, 8, BLK), i32),
             smem((DOM, 8, BLK), i32),
-            vmem((8, 384), i32),
-            smem((8, 384), i32),
+            vmem((12, 384), i32),
+            smem((12, 384), i32),
             vmem((FORWARD_PAIRS + 1, BLK, D), f32),
             vmem(blocks, bf16),
+            vmem(blocks, f32),
             vmem(blocks, bf16),
             vmem((DOM, 8, 2, 16, BLK), bf16),
             vmem((DOM, 8, 16, BLK), bf16),
             vmem((8, DOM, 16, BLK), bf16),
-            vmem(blocks, f32),
             vmem((D, D), f32),
-            vmem((GRP, 16, D), f32),
-            vmem((GRP, 16, D), f32),
+            vmem((GRP, 16, D), bf16),
+            vmem((GRP, 16, D), bf16),
             vmem((16, D), f32),
             vmem((DOM, 16, D), f32),
-            vmem((16, D), f32),
+            vmem((16, D), WEIGHT_SUM),
             dma((11,)),
             dma((22,)),
         ],
@@ -442,15 +480,21 @@
         send_rows,
         jnp.swapaxes(cache_ask.reshape(DOM, 2), 0, 1),
     )
-    whole = pl.BlockSpec(memory_space=vmem)
-    part = pl.BlockSpec((FINISH_BLOCKS, BLK, D), lambda i: (i, 0, 0))
     grad_inputs, layer_out, grad_weight = pl.pallas_call(
         finish,
-        grid=(ROW_BLOCKS // FINISH_BLOCKS,),
         out_shape=(shape(blocks, f32), shape(blocks, bf16), shape((GRP, 16, D), f32)),
-        in_specs=[whole, part, part, whole, whole],
-        out_specs=(part, part, whole),
-        scratch_shapes=[vmem((1024, D), bf16), vmem((1, 1024), i32)],
+        in_specs=[hbm] * 5,
+        out_specs=(hbm,) * 3,
+        scratch_shapes=[
+            vmem((8, 128), i32),
+            vmem(blocks, f32),
+            vmem(blocks, bf16),
+            vmem((GRP, 16, D), WEIGHT_SUM),
+            vmem(back_home, bf16),
+            vmem(blocks, f32),
+            vmem((GRP, 16, D), f32),
+            dma((4 + ROW_BLOCKS // FINISH_BLOCKS,)),
+        ],
         compiler_params=pltpu.CompilerParams(vmem_limit_bytes=60 * 1024 * 1024),
     )(send_rows, own_grads, layer_out, grad_weight, returned)
     rows = ROW_BLOCKS * BLK

time: 60.6 us -> 58.7 us (0.969)
  Pallas kernels: 59.1 us -> 57.2 us
    pallas_call x1, Pallas kernels: 7.35 us -> 4.89 us  [per_device(): pl.pallas_call(finish, out_shape=(shape(blocks, f32), shape(blocks, bf16)...]
    pallas_call x1, Pallas kernels: 51.7 us -> 52.3 us  [per_device(): pl.pallas_call(kernel, out_shape=(shape(blocks, bf16), shape(blocks, f32)...]
where the time goes in v3:
time: 58.7 us; the launch traced here: 58.5 us
  Pallas kernels  57.2 us (97%)
  between operations  1.29 us (2%)
    pallas_call x1, Pallas kernels, per_device(): pl.pallas_call(kernel, out_shape=(shape(blocks, bf16), shape(blocks, f32)...  52.3 us
    pallas_call x1, Pallas kernels, per_device(): pl.pallas_call(finish, out_shape=(shape(blocks, f32), shape(blocks, bf16)...  4.89 us

profile of v3, /device:TPU:1, one launch (start us, length us, event | category | flops | bytes accessed | tf_op | source)
XLA Modules:
  0.0 58.5 jit_solution(366016237409357163)
XLA Ops:
  1.3 52.3 %shard_map.130 = (bf16[24,128,256]{2,1,0:T(8,128)(2,1)}, f32[24,128,256]{2,1,0:T(8,128)}, bf16[8,8,2,16,128]{4,3,2,1,0:T(8,128)(2,1)}, f32[16,16,256]{2,1,0:T(8,128)}) custom-call(bf16[24,128,256]{2,1,0:T(8,128)(2,1)} %bitcast.13, bf16[24,128,256]{2,1,0:T(8,128)(2,1)} %bitcast.14, bf16[24,128,256]{2,1,0:T(8,128)(2,1)} %bitcast.15, ...), custom_call_target="tpu_custom_call" | custom-call | tf_op jit(solution)/shard_map/pallas_call | solution.py:425
  53.6 4.9 %shard_map.131 = (f32[24,128,256]{2,1,0:T(8,128)}, bf16[24,128,256]{2,1,0:T(8,128)(2,1)}, f32[16,16,256]{2,1,0:T(8,128)}) custom-call(s32[8,128]{1,0:T(8,128)} %bitcast.18, f32[24,128,256]{2,1,0:T(8,128)} %get-tuple-element.10.own, bf16[24,128,256]{2,1,0:T(8,128)(2,1)} %get-tuple-element.11.layer, f32[16,16,256]{2,1,0:T(8,128)} %get-tuple-element.12.weight_in, ...), custom_call_target="tpu_custom_call" | custom-call | tf_op jit(solution)/shard_map/pallas_call | solution.py:483

commit v4 on v3

--- a/solution.py
+++ b/solution.py
@@ -29,7 +29,7 @@
 MIDDLE_BLOCKS = 8
 FINISH_BLOCKS = 12
 DROPPED = 200
-WEIGHT_SUM = f32
+WEIGHT_SUM = bf16
 
 
 def each(count, visit, first=1):
@@ -96,7 +96,7 @@
         out[i : i + 1, :] = v
 
 
-def run_pairs(lists, base, steps, unroll, product, sums):
+def run_pairs(lists, base, steps, unroll, product, sums, first=0, running=None):
     def body(s, running):
         for u in range(unroll):
             q = s * unroll + u
@@ -106,7 +106,8 @@
             sums[q] = running
         return running
 
-    lax.fori_loop(0, steps // unroll, body, jnp.zeros((BLK, D), f32))
+    running = jnp.zeros((BLK, D), f32) if running is None else running
+    return lax.fori_loop(first // unroll, steps // unroll, body, running)
 
 
 def listed_rows(listed, group):
@@ -288,7 +289,7 @@
     lax.fori_loop(0, ROW_BLOCKS // MIDDLE_BLOCKS, middle, 0)
     put_layer = load(0, layer_v, layer_out)
 
-    part_out[...] = weight_part[...].astype(bf16).reshape(GRP, 16, D)
+    part_out[...] = weight_part[...].reshape(GRP, 16, D)
     each(GRP, lambda i: push(part_out.at[grp_peer(i)], part_in.at[g], 8, (d, grp_peer(i))))
     keep(part_out.at[g], part_in.at[g], 8)
 
@@ -317,12 +318,15 @@
 
     lax.fori_loop(0, 8, over_grp, 0)
 
+    half_own = OWN_PAIRS // 2
+    running = run_pairs(lists, 8, half_own, OWN_UNROLL, spread_product, sums)
+
     landed(part_in, 8)
-    group_sum[...] = jnp.sum(part_in[...].astype(f32), axis=0)
+    group_sum[...] = jnp.sum(part_in[...], axis=0)
     each(DOM, lambda i: push(group_sum, dom_in.at[d], 14, (dom_peer(i), g)))
     keep(group_sum, dom_in.at[d], 14)
 
-    run_pairs(lists, 8, OWN_PAIRS, OWN_UNROLL, spread_product, sums)
+    run_pairs(lists, 8, OWN_PAIRS, OWN_UNROLL, spread_product, sums, half_own, running)
 
     landed(turn_a, 10)
     home = returned.at[:, half, parity]
@@ -456,8 +460,8 @@
             vmem((DOM, 8, 16, BLK), bf16),
             vmem((8, DOM, 16, BLK), bf16),
             vmem((D, D), f32),
-            vmem((GRP, 16, D), bf16),
-            vmem((GRP, 16, D), bf16),
+            vmem((GRP, 16, D), f32),
+            vmem((GRP, 16, D), f32),
             vmem((16, D), f32),
             vmem((DOM, 16, D), f32),
             vmem((16, D), WEIGHT_SUM),

time: 58.7 us -> 56.5 us (0.963)
  Pallas kernels: 57.2 us -> 55 us
    pallas_call x1, Pallas kernels: 52.3 us -> 50.1 us  [per_device(): pl.pallas_call(kernel, out_shape=(shape(blocks, bf16), shape(blocks, f32)...]
where the time goes in v4:
time: 56.5 us; the launch traced here: 56.2 us
  Pallas kernels  55 us (97%)
  between operations  1.29 us (2%)
    pallas_call x1, Pallas kernels, per_device(): pl.pallas_call(kernel, out_shape=(shape(blocks, bf16), shape(blocks, f32)...  50.1 us
    pallas_call x1, Pallas kernels, per_device(): pl.pallas_call(finish, out_shape=(shape(blocks, f32), shape(blocks, bf16)...  4.9 us

profile of v4, /device:TPU:1, one launch (start us, length us, event | category | flops | bytes accessed | tf_op | source)
XLA Modules:
  0.0 56.2 jit_solution(3775795145019350041)
XLA Ops:
  1.3 50.1 %shard_map.130 = (bf16[24,128,256]{2,1,0:T(8,128)(2,1)}, f32[24,128,256]{2,1,0:T(8,128)}, bf16[8,8,2,16,128]{4,3,2,1,0:T(8,128)(2,1)}, bf16[16,16,256]{2,1,0:T(8,128)(2,1)}) custom-call(bf16[24,128,256]{2,1,0:T(8,128)(2,1)} %bitcast.13, bf16[24,128,256]{2,1,0:T(8,128)(2,1)} %bitcast.14, bf16[24,128,256]{2,1,0:T(8,128)(2,1)} %bitcast.15, ...), custom_call_target="tpu_custom_call" | custom-call | tf_op jit(solution)/shard_map/pallas_call | solution.py:429
  51.3 4.9 %shard_map.131 = (f32[24,128,256]{2,1,0:T(8,128)}, bf16[24,128,256]{2,1,0:T(8,128)(2,1)}, f32[16,16,256]{2,1,0:T(8,128)}) custom-call(s32[8,128]{1,0:T(8,128)} %bitcast.18, f32[24,128,256]{2,1,0:T(8,128)} %get-tuple-element.10.own, bf16[24,128,256]{2,1,0:T(8,128)(2,1)} %get-tuple-element.11.layer, bf16[16,16,256]{2,1,0:T(8,128)(2,1)} %get-tuple-element.12.weight_in, ...), custom_call_target="tpu_custom_call" | custom-call | tf_op jit(solution)/shard_map/pallas_call | solution.py:487

commit v5 on v4

--- a/solution.py
+++ b/solution.py
@@ -25,7 +25,7 @@
 FRESH_PAIRS = (TILES - COLUMNS + 2 * FRESH) // 2
 OWN_PAIRS = (TILES - COLUMNS + 2 * ROW_BLOCKS) // 2
 NO_SUM = FORWARD_PAIRS
-FORWARD_UNROLL, FRESH_UNROLL, OWN_UNROLL = 78, 64, 72
+FORWARD_UNROLL, FRESH_UNROLL, OWN_UNROLL = 78, 128, 72
 MIDDLE_BLOCKS = 8
 FINISH_BLOCKS = 12
 DROPPED = 200

time: 56.5 us -> 56.2 us (level)
  no operation moved by 1% of the time
where the time goes in v5:
time: 56.2 us; the launch traced here: 55.9 us
  Pallas kernels  54.6 us (97%)
  between operations  1.29 us (2%)
    pallas_call x1, Pallas kernels, per_device(): pl.pallas_call(kernel, out_shape=(shape(blocks, bf16), shape(blocks, f32)...  49.7 us
    pallas_call x1, Pallas kernels, per_device(): pl.pallas_call(finish, out_shape=(shape(blocks, f32), shape(blocks, bf16)...  4.9 us

profile of v5, /device:TPU:1, one launch (start us, length us, event | category | flops | bytes accessed | tf_op | source)
XLA Modules:
  0.0 55.9 jit_solution(9572463708449861281)
XLA Ops:
  1.3 49.7 %shard_map.130 = (bf16[24,128,256]{2,1,0:T(8,128)(2,1)}, f32[24,128,256]{2,1,0:T(8,128)}, bf16[8,8,2,16,128]{4,3,2,1,0:T(8,128)(2,1)}, bf16[16,16,256]{2,1,0:T(8,128)(2,1)}) custom-call(bf16[24,128,256]{2,1,0:T(8,128)(2,1)} %bitcast.13, bf16[24,128,256]{2,1,0:T(8,128)(2,1)} %bitcast.14, bf16[24,128,256]{2,1,0:T(8,128)(2,1)} %bitcast.15, ...), custom_call_target="tpu_custom_call" | custom-call | tf_op jit(solution)/shard_map/pallas_call | solution.py:429
  51.0 4.9 %shard_map.131 = (f32[24,128,256]{2,1,0:T(8,128)}, bf16[24,128,256]{2,1,0:T(8,128)(2,1)}, f32[16,16,256]{2,1,0:T(8,128)}) custom-call(s32[8,128]{1,0:T(8,128)} %bitcast.18, f32[24,128,256]{2,1,0:T(8,128)} %get-tuple-element.10.own, bf16[24,128,256]{2,1,0:T(8,128)(2,1)} %get-tuple-element.11.layer, bf16[16,16,256]{2,1,0:T(8,128)(2,1)} %get-tuple-element.12.weight_in, ...), custom_call_target="tpu_custom_call" | custom-call | tf_op jit(solution)/shard_map/pallas_call | solution.py:487
